TPU v7x, 1024 devices: a whole 4x4x32 slice. The times are simulated.
1024 devices in a mesh: dp: 64 (over z, core), seq: 16 (over y, x).
Axes of the slice: x: 4, y: 4, z: 32, core: 2. Of those that a mesh axis runs over, the one named last changes fastest.
Arguments:
- queries: bfloat16 [131072, 4096], P(('dp', 'seq')), may hold values from -30 to 30, as said below
- keys: bfloat16 [131072, 512], P(('dp', 'seq')), may hold values from -30 to 30, as said below
- values: bfloat16 [131072, 512], P(('dp', 'seq')), may hold values from -6 to 6
- starts: int32 [131072], P(('dp', 'seq')), may hold values from 0 to 131071, as said below
Outputs:
- attended: bfloat16 [131072, 4096], P(('dp', 'seq'))
Inputs may be any that keep to these rules, and one draw needn't show every extreme that they name: starts never decrease along the tokens (starts[t] <= starts[t+1]); starts[t] <= t and t - starts[t] < 1024; all tokens from starts[t] to t share t's start; some sequence is exactly 1024 tokens long. `queries`: entries stay within -30 to 30. `keys`: entries stay within -30 to 30.
All inputs are finite; a program needn't handle non-finite values.
Results may differ from a plain program's by a relative error of at most 0.0035.
Values may be sent and summed in bfloat16 or wider, within the bound.
No kernel may reach another device: no remote copies, remote signals or barrier semaphores. Data moves between devices by JAX's collectives and lax.ppermute only.
A program may use at most 32 MiB of HBM per device.

v0:
```python
import functools
import math

import jax
import jax.numpy as jnp
from jax import lax
from jax.experimental import pallas as pl
from jax.experimental.pallas import tpu as pltpu
from jax.sharding import PartitionSpec as P

HQ = 32
HK = 4
DH = 128
GROUP = HQ // HK
AXES = ("dp", "seq")
SIDE = 4
SCALE = math.log2(math.e) * DH**-0.5
MASKED = -1e30


def shift(block, distance):
    n = lax.axis_size(AXES)
    return lax.ppermute(block, AXES, [(i, i + distance) for i in range(n - distance)])


def attend(distances, chunk, merge, final, *refs):
    starts_ref, q_ref, *refs = refs
    if final:
        flag_ref, *refs = refs
    arrays = len(distances) + final
    kv_refs, refs = refs[:arrays], refs[arrays:]
    if merge:
        acc_in, top_in, total_in, *refs = refs
    if final:
        out_ref, done_ref, sems, *refs = refs
    else:
        acc_out, top_out, total_out, *refs = refs
    bias_ref, k_ref, v_ref = refs
    tok = q_ref.shape[0]
    flat = [d for group in distances for d in group]
    width = len(flat) * tok
    first = jnp.broadcast_to(starts_ref[...].astype(jnp.float32), (tok, tok)).T
    column = lax.broadcasted_iota(jnp.int32, (tok, tok), 1).astype(jnp.float32)
    row = lax.broadcasted_iota(jnp.int32, (tok, tok), 0).astype(jnp.float32)
    for i, d in enumerate(flat):
        allowed = column - float(tok * d) >= first
        if d == 0:
            allowed = allowed & (column <= row)
        bias_ref[:, i * tok : (i + 1) * tok] = jnp.where(allowed, 0.0, MASKED)
    v_ref[:, :, DH:] = jnp.ones((HK, width, DH), v_ref.dtype)

    def fill(kv_refs):
        for g in range(HK):
            lanes = slice(g * DH, (g + 1) * DH)
            i = 0
            for group, kv_ref in zip(distances, kv_refs):
                for j in range(len(group)):
                    to = slice(i * tok, (i + 1) * tok)
                    k_ref[g, to] = kv_ref[2 * j * tok : (2 * j + 1) * tok, lanes]
                    v_ref[g, to, :DH] = kv_ref[(2 * j + 1) * tok : (2 * j + 2) * tok, lanes]
                    i += 1

    if final:
        pl.when(flag_ref[0] != 0)(lambda: fill(kv_refs[1:]))
        pl.when(flag_ref[0] == 0)(lambda: fill(kv_refs[:-1]))
    else:
        fill(kv_refs)

    def heads_of(ref, heads):
        return jnp.concatenate([ref[:, h * DH : (h + 1) * DH] for h in heads], axis=0)

    copies = []
    for c in range(0, HQ, chunk):
        g = c // GROUP
        heads = range(c, c + chunk)
        scores = lax.dot_general(
            heads_of(q_ref, heads),
            k_ref[g],
            (((1,), (1,)), ((), ())),
            preferred_element_type=jnp.float32,
        )
        scores = scores.reshape(chunk, tok, width) * SCALE + bias_ref[...][None]
        scores = scores.reshape(chunk * tok, width)
        top = jnp.max(scores, axis=1, keepdims=True)
        top = jnp.broadcast_to(top, (chunk * tok, DH))
        if merge:
            top_old = heads_of(top_in, heads)
            top = jnp.maximum(top, top_old)
        tops = jnp.concatenate([top] * len(flat), axis=1)
        weights = jnp.exp2(scores - tops).astype(jnp.bfloat16)
        mixed = jnp.dot(weights, v_ref[g], preferred_element_type=jnp.float32)
        mixed, total = mixed[:, :DH], mixed[:, DH:]
        if merge:
            fade = jnp.exp2(top_old - top)
            mixed = mixed + heads_of(acc_in, heads) * fade
            total = total + heads_of(total_in, heads) * fade
        if final:
            mixed = (mixed / total).astype(done_ref.dtype)
        for n, h in enumerate(heads):
            rows, lanes = slice(n * tok, (n + 1) * tok), slice(h * DH, (h + 1) * DH)
            if final:
                done_ref[:, lanes] = mixed[rows]
            else:
                acc_out[:, lanes] = mixed[rows]
                top_out[:, lanes] = top[rows]
                total_out[:, lanes] = total[rows]
        if final:
            lanes = pl.ds(c * DH, chunk * DH)
            copy = pltpu.make_async_copy(
                done_ref.at[:, lanes], out_ref.at[:, lanes], sems.at[c // chunk]
            )
            copy.start()
            copies.append(copy)
    for copy in copies:
        copy.wait()


def attention(starts, queries, arrays, distances, state=None, flag=None, chunk=4):
    tok = queries.shape[0]
    blocks = sum(len(group) for group in distances)
    final = flag is not None
    operands = [starts.reshape(1, tok), queries, *([flag] if final else [])]
    in_specs = [pl.BlockSpec(memory_space=pltpu.VMEM)] * 2
    in_specs += [pl.BlockSpec(memory_space=pltpu.SMEM)] * final
    operands += [*arrays, *(state or [])]
    in_specs += [pl.BlockSpec(memory_space=pltpu.VMEM)] * (len(operands) - len(in_specs))
    scratch = [
        pltpu.VMEM((tok, blocks * tok), jnp.float32),
        pltpu.VMEM((HK, blocks * tok, DH), jnp.bfloat16),
        pltpu.VMEM((HK, blocks * tok, 2 * DH), jnp.bfloat16),
    ]
    aliases = {}
    if final:
        out_shape = jax.ShapeDtypeStruct(queries.shape, queries.dtype)
        out_specs = pl.BlockSpec(memory_space=pl.ANY)
        scratch = [
            pltpu.VMEM(queries.shape, queries.dtype),
            pltpu.SemaphoreType.DMA((HQ // chunk,)),
        ] + scratch
    else:
        out_shape = [jax.ShapeDtypeStruct(queries.shape, jnp.float32)] * 3
        out_specs = [pl.BlockSpec(memory_space=pltpu.VMEM)] * 3
        if state is not None:
            aliases = {len(operands) - 3 + i: i for i in range(3)}
    return pl.pallas_call(
        functools.partial(attend, distances, chunk, state is not None, final),
        in_specs=in_specs,
        out_specs=out_specs,
        out_shape=out_shape,
        scratch_shapes=scratch,
        input_output_aliases=aliases,
        compiler_params=pltpu.CompilerParams(vmem_limit_bytes=16 * 2**20),
        cost_estimate=pl.CostEstimate(
            flops=4 * HQ * tok * blocks * tok * DH,
            bytes_accessed=(2 * HQ + 4 * HK * blocks) * tok * DH * 2,
            transcendentals=HQ * tok * blocks * tok,
        ),
    )(*operands)


def turn(block, columns):
    n = lax.axis_size("seq")
    route = [(i, i // SIDE * SIDE + (i + columns) % SIDE) for i in range(n)]
    return lax.ppermute(block, "seq", route)


def over(first, second):
    zero, n = jnp.zeros((), first.dtype), first.shape[0]
    return lax.pad(first, zero, ((0, n, 0), (0, 0, 0))) + lax.pad(
        second, zero, ((n, 0, 0), (0, 0, 0))
    )


def shards(queries, keys, values, starts):
    tok = queries.shape[0]
    seq = lax.axis_index("seq")
    me = lax.axis_index("dp") * lax.axis_size("seq") + seq
    column = seq % SIDE
    kv = over(keys, values)
    kv4 = shift(kv, SIDE)
    kv8 = shift(kv, 2 * SIDE)
    across = turn(kv, 2)
    across4 = shift(across, SIDE)
    across8 = shift(across, 2 * SIDE)
    held = jnp.concatenate([kv, kv4, kv8], axis=0)

    def pair(columns):
        wraps = column + columns >= SIDE
        return lax.dynamic_slice_in_dim(held, jnp.where(wraps, 2 * tok, 0), 4 * tok, 0)

    kv15 = turn(pair(1), 1)
    kv37 = turn(pair(3), 3)
    starts = starts - me * tok
    state = attention(starts, queries, [kv, kv4, kv8], [(0,), (4,), (8,)])
    state = attention(starts, queries, [kv15, kv37], [(1, 5), (3, 7)], state=state, chunk=2)
    early = (column < 2).astype(jnp.int32).reshape(1)
    return attention(
        starts, queries, [across, across4, across8], [(2,), (6,)], state=state, flag=early
    )


def solution(mesh):
    return jax.shard_map(
        shards,
        mesh=mesh,
        in_specs=(P(AXES, None), P(AXES, None), P(AXES, None), P(AXES)),
        out_specs=P(AXES, None),
        check_vma=False,
    )
```

profile of v0, /device:TPU:8, one launch (start us, length us, event | category | flops | bytes accessed | tf_op | source)
XLA Modules:
  0.0 46.9 jit_solution(7942270813587276522)
XLA Ops:
  0.0 0.0 copy-start.3
  0.0 0.0 copy-start
  0.0 1.1 %pad_add_fusion.refs_2_ = bf16[256,512]{1,0:T(8,128)(2,1)S(1)} fusion(bf16[128,512]{1,0:T(8,128)(2,1)} %param.6, bf16[128,512]{1,0:T(8,128)(2,1)} %param.5), kind=kLoop, calls=%fused_computation.1 | loop fusion | flops 524288 | bytes 524288 | tf_op jit(solution)/shard_map/add | solution.py:169
  1.1 3.5 %collective-permute-start.3 = (bf16[256,512]{1,0:T(8,128)(2,1)S(1)}, bf16[256,512]{1,0:T(8,128)(2,1)S(1)}, u32[]{:S(2)}, u32[]{:S(2)}) collective-permute-start(bf16[256,512]{1,0:T(8,128)(2,1)S(1)} %pad_add_fusion.refs_2_), channel_id=1, source_target_pairs={{0,4},{1,5},{2,6},{3,7},{4,8},{5,9},{6,10},{7,11},{8,12},{9,13},{1... | collective-permute-start | bytes 786440 | tf_op jit(solution)/shard_map/ppermute | solution.py:23
  4.6 2.7 %collective-permute-start.4 = (bf16[256,512]{1,0:T(8,128)(2,1)S(1)}, bf16[256,512]{1,0:T(8,128)(2,1)S(1)}, u32[]{:S(2)}, u32[]{:S(2)}) collective-permute-start(bf16[256,512]{1,0:T(8,128)(2,1)S(1)} %pad_add_fusion.refs_2_), channel_id=1, source_target_pairs={{0,8},{1,9},{2,10},{3,11},{4,12},{5,13},{6,14},{7,15},{8,16},{9,17... | collective-permute-start | bytes 786440 | tf_op jit(solution)/shard_map/ppermute | solution.py:23
  7.2 4.9 %collective-permute-start = (bf16[256,512]{1,0:T(8,128)(2,1)S(1)}, bf16[256,512]{1,0:T(8,128)(2,1)S(1)}, u32[]{:S(2)}, u32[]{:S(2)}) collective-permute-start(bf16[256,512]{1,0:T(8,128)(2,1)S(1)} %pad_add_fusion.refs_2_), channel_id=1, source_target_pairs={{0,2},{1,3},{2,0},{3,1},{4,6},{5,7},{6,4},{7,5},{8,10},{9,11},{10,... | collective-permute-start | bytes 786440 | tf_op jit(solution)/shard_map/ppermute | solution.py:164
  12.2 7.6 %collective-permute-done.3.refs_3_ = bf16[256,512]{1,0:T(8,128)(2,1)S(1)} collective-permute-done((bf16[256,512]{1,0:T(8,128)(2,1)S(1)}, bf16[256,512]{1,0:T(8,128)(2,1)S(1)}, u32[]{:S(2)}, u32[]{:S(2)}) %collective-permute-start.3) | collective-permute-done | bytes 262176 | tf_op jit(solution)/shard_map/ppermute | solution.py:23
  19.8 0.0 collective-permute-done.4.refs_4_
  19.8 0.0 copy-start.1
  19.8 0.1 pad_maximum_fusion
  19.9 1.0 %constant_dynamic-slice_fusion = (bf16[512,512]{1,0:T(8,128)(2,1)}, bf16[512,512]{1,0:T(8,128)(2,1)}) fusion(bf16[768,512]{1,0:T(8,128)(2,1)S(1)} %pad_maximum_fusion, s32[]{:T(128)S(6)} %select_n.18, s32[]{:T(128)S(6)} %select_n.17), kind=kLoop, calls=%fused_computation.2 | loop fusion | bytes 2097160 | tf_op jit(solution)/shard_map/dynamic_slice | solution.py:189
  20.9 1.9 %collective-permute-start.5 = (bf16[512,512]{1,0:T(8,128)(2,1)}, bf16[512,512]{1,0:T(8,128)(2,1)S(1)}, u32[]{:S(2)}, u32[]{:S(2)}) collective-permute-start(bf16[512,512]{1,0:T(8,128)(2,1)} %get-tuple-element.18), channel_id=1, source_target_pairs={{0,1},{1,2},{2,3},{3,0},{4,5},{5,6},{6,7},{7,4},{8,9},{9,10},{10,1... | collective-permute-start | bytes 1572872 | tf_op jit(solution)/shard_map/ppermute | solution.py:164
  22.8 5.1 %collective-permute-start.6 = (bf16[512,512]{1,0:T(8,128)(2,1)}, bf16[512,512]{1,0:T(8,128)(2,1)S(1)}, u32[]{:S(2)}, u32[]{:S(2)}) collective-permute-start(bf16[512,512]{1,0:T(8,128)(2,1)} %get-tuple-element.17), channel_id=1, source_target_pairs={{0,3},{1,0},{2,1},{3,2},{4,7},{5,4},{6,5},{7,6},{8,11},{9,8},{10,9... | collective-permute-start | bytes 1572872 | tf_op jit(solution)/shard_map/ppermute | solution.py:164
  28.0 0.0 copy-done.1
  28.0 0.0 collective-permute-done.refs_3_
  28.0 6.2 %collective-permute-start.1 = (bf16[256,512]{1,0:T(8,128)(2,1)S(1)}, bf16[256,512]{1,0:T(8,128)(2,1)S(1)}, u32[]{:S(2)}, u32[]{:S(2)}) collective-permute-start(bf16[256,512]{1,0:T(8,128)(2,1)S(1)} %collective-permute-done.refs_3_), channel_id=1, source_target_pairs={{0,4},{1,5},{2,6},{3,7},{4,8},{5,9},{6,10},{7,11},{8,12},{9,13},{1... | collective-permute-start | bytes 786440 | tf_op jit(solution)/shard_map/ppermute | solution.py:23
  34.2 1.3 %collective-permute-start.2 = (bf16[256,512]{1,0:T(8,128)(2,1)S(1)}, bf16[256,512]{1,0:T(8,128)(2,1)S(1)}, u32[]{:S(2)}, u32[]{:S(2)}) collective-permute-start(bf16[256,512]{1,0:T(8,128)(2,1)S(1)} %collective-permute-done.refs_3_), channel_id=1, source_target_pairs={{0,8},{1,9},{2,10},{3,11},{4,12},{5,13},{6,14},{7,15},{8,16},{9,17... | collective-permute-start | bytes 786440 | tf_op jit(solution)/shard_map/ppermute | solution.py:23
  35.5 0.0 copy-done.3
  35.5 0.0 copy-done
  35.5 0.0 copy-start.2
  35.5 0.9 %copy-done.2 = bf16[256,512]{1,0:T(8,128)(2,1)S(1)} copy-done((bf16[256,512]{1,0:T(8,128)(2,1)S(1)}, bf16[256,512]{1,0:T(8,128)(2,1)}, u32[]{:S(2)}) %copy-start.2) | copy-done | bytes 262168
  36.5 3.3 %shard_map.46 = (f32[128,4096]{1,0:T(8,128)S(1)}, f32[128,4096]{1,0:T(8,128)S(1)}, f32[128,4096]{1,0:T(8,128)S(1)}) custom-call(s32[1,128]{1,0:T(1,128)S(1)} %subtract_bitcast_fusion.refs_0_, bf16[128,4096]{1,0:T(8,128)(2,1)S(1)} %copy-done, bf16[256,512]{1,0:T(8,128)(2,1)S(1)} %pad_add_fusion.refs_2_, bf16[256,512]{1,0:T(8,128)(2,1)S(1)} %collective-permute-done.3.refs_3_, ...), custom_call_target="tpu_custom_call" | custom-call | flops 805306368 | bytes 3670016 | tf_op jit(solution)/shard_map/pallas_call | solution.py:145
  39.8 0.0 collective-permute-done.5.refs_2_
  39.9 0.0 collective-permute-done.6.refs_3_
  39.9 4.1 %shard_map.47 = (f32[128,4096]{1,0:T(8,128)S(1)}, f32[128,4096]{1,0:T(8,128)S(1)}, f32[128,4096]{1,0:T(8,128)S(1)}) custom-call(s32[1,128]{1,0:T(1,128)S(1)} %subtract_bitcast_fusion.refs_0_, bf16[128,4096]{1,0:T(8,128)(2,1)S(1)} %copy-done, ...), custom_call_target="tpu_custom_call", output_to_operand_aliasing={{0}: (4, {}), {1}: (5, {}), {2}: (6, {})} | custom-call | flops 1073741824 | bytes 4194304 | tf_op jit(solution)/shard_map/pallas_call | solution.py:145
  44.0 0.0 collective-permute-done.1.refs_4_
  44.0 0.0 collective-permute-done.2.refs_5_
  44.0 2.9 %shard_map.48 = bf16[128,4096]{1,0:T(8,128)(2,1)} custom-call(s32[1,128]{1,0:T(1,128)S(1)} %subtract_bitcast_fusion.refs_0_, bf16[128,4096]{1,0:T(8,128)(2,1)S(1)} %copy-done, s32[1]{0:T(128)} %bitcast.1.refs_2_, bf16[256,512]{1,0:T(8,128)(2,1)S(1)} %collective-permute-done.refs_3_, bf16[256,512]{1,0:T(8,128)(2,1)S(1)} %collective-permute-done.1.refs_4_, ...), custom_call_target="tpu_custom_call" | custom-call | flops 536870912 | bytes 3145728 | tf_op jit(solution)/shard_map/pallas_call | solution.py:145
  (1 shorter events, 0.0 us)
Async XLA Ops:
  0.0 35.5 %copy-start.3 = (s32[128]{0:T(128)S(1)}, s32[128]{0:T(128)}, u32[]{:S(2)}) copy-start(s32[128]{0:T(128)} %param.7) | copy-start | bytes 1540
  0.0 35.5 %copy-start = (bf16[128,4096]{1,0:T(8,128)(2,1)S(1)}, bf16[128,4096]{1,0:T(8,128)(2,1)}, u32[]{:S(2)}) copy-start(bf16[128,4096]{1,0:T(8,128)(2,1)} %refs_1_.5) | copy-start | bytes 3145732
  1.1 18.7 %collective-permute-start.3 = (bf16[256,512]{1,0:T(8,128)(2,1)S(1)}, bf16[256,512]{1,0:T(8,128)(2,1)S(1)}, u32[]{:S(2)}, u32[]{:S(2)}) collective-permute-start(bf16[256,512]{1,0:T(8,128)(2,1)S(1)} %pad_add_fusion.refs_2_), channel_id=1, source_target_pairs={{0,4},{1,5},{2,6},{3,7},{4,8},{5,9},{6,10},{7,11},{8,12},{9,13},{1... | collective-permute-start | bytes 786440 | tf_op jit(solution)/shard_map/ppermute | solution.py:23
  4.6 15.2 %collective-permute-start.4 = (bf16[256,512]{1,0:T(8,128)(2,1)S(1)}, bf16[256,512]{1,0:T(8,128)(2,1)S(1)}, u32[]{:S(2)}, u32[]{:S(2)}) collective-permute-start(bf16[256,512]{1,0:T(8,128)(2,1)S(1)} %pad_add_fusion.refs_2_), channel_id=1, source_target_pairs={{0,8},{1,9},{2,10},{3,11},{4,12},{5,13},{6,14},{7,15},{8,16},{9,17... | collective-permute-start | bytes 786440 | tf_op jit(solution)/shard_map/ppermute | solution.py:23
  7.2 20.8 %collective-permute-start = (bf16[256,512]{1,0:T(8,128)(2,1)S(1)}, bf16[256,512]{1,0:T(8,128)(2,1)S(1)}, u32[]{:S(2)}, u32[]{:S(2)}) collective-permute-start(bf16[256,512]{1,0:T(8,128)(2,1)S(1)} %pad_add_fusion.refs_2_), channel_id=1, source_target_pairs={{0,2},{1,3},{2,0},{3,1},{4,6},{5,7},{6,4},{7,5},{8,10},{9,11},{10,... | collective-permute-start | bytes 786440 | tf_op jit(solution)/shard_map/ppermute | solution.py:164
  19.8 8.2 %copy-start.1 = (bf16[256,512]{1,0:T(8,128)(2,1)}, bf16[256,512]{1,0:T(8,128)(2,1)S(1)}, u32[]{:S(2)}) copy-start(bf16[256,512]{1,0:T(8,128)(2,1)S(1)} %collective-permute-done.4.refs_4_) | copy-start | bytes 786436
  20.9 18.9 %collective-permute-start.5 = (bf16[512,512]{1,0:T(8,128)(2,1)}, bf16[512,512]{1,0:T(8,128)(2,1)S(1)}, u32[]{:S(2)}, u32[]{:S(2)}) collective-permute-start(bf16[512,512]{1,0:T(8,128)(2,1)} %get-tuple-element.18), channel_id=1, source_target_pairs={{0,1},{1,2},{2,3},{3,0},{4,5},{5,6},{6,7},{7,4},{8,9},{9,10},{10,1... | collective-permute-start | bytes 1572872 | tf_op jit(solution)/shard_map/ppermute | solution.py:164
  22.8 17.0 %collective-permute-start.6 = (bf16[512,512]{1,0:T(8,128)(2,1)}, bf16[512,512]{1,0:T(8,128)(2,1)S(1)}, u32[]{:S(2)}, u32[]{:S(2)}) collective-permute-start(bf16[512,512]{1,0:T(8,128)(2,1)} %get-tuple-element.17), channel_id=1, source_target_pairs={{0,3},{1,0},{2,1},{3,2},{4,7},{5,4},{6,5},{7,6},{8,11},{9,8},{10,9... | collective-permute-start | bytes 1572872 | tf_op jit(solution)/shard_map/ppermute | solution.py:164
  28.0 16.0 %collective-permute-start.1 = (bf16[256,512]{1,0:T(8,128)(2,1)S(1)}, bf16[256,512]{1,0:T(8,128)(2,1)S(1)}, u32[]{:S(2)}, u32[]{:S(2)}) collective-permute-start(bf16[256,512]{1,0:T(8,128)(2,1)S(1)} %collective-permute-done.refs_3_), channel_id=1, source_target_pairs={{0,4},{1,5},{2,6},{3,7},{4,8},{5,9},{6,10},{7,11},{8,12},{9,13},{1... | collective-permute-start | bytes 786440 | tf_op jit(solution)/shard_map/ppermute | solution.py:23
  34.2 9.8 %collective-permute-start.2 = (bf16[256,512]{1,0:T(8,128)(2,1)S(1)}, bf16[256,512]{1,0:T(8,128)(2,1)S(1)}, u32[]{:S(2)}, u32[]{:S(2)}) collective-permute-start(bf16[256,512]{1,0:T(8,128)(2,1)S(1)} %collective-permute-done.refs_3_), channel_id=1, source_target_pairs={{0,8},{1,9},{2,10},{3,11},{4,12},{5,13},{6,14},{7,15},{8,16},{9,17... | collective-permute-start | bytes 786440 | tf_op jit(solution)/shard_map/ppermute | solution.py:23
  35.5 1.0 %copy-start.2 = (bf16[256,512]{1,0:T(8,128)(2,1)S(1)}, bf16[256,512]{1,0:T(8,128)(2,1)}, u32[]{:S(2)}) copy-start(bf16[256,512]{1,0:T(8,128)(2,1)} %copy-done.1) | copy-start | bytes 786436
where the time goes:
time: 47.2 us; the launch traced here: 46.9 us
  starting transfers between devices  25.6 us (54%)
  Pallas kernels  10.4 us (22%)
  waiting for transfers between devices  7.63 us (16%)
  local copies, waits for them, and re-layouts  2 us (4%)
  other arithmetic  1.13 us (2%)
    ppermute x4, starting transfers between devices, shift(): lax.ppermute(block, AXES, [(i, i + distance) for i in range(n - distance)])  13.6 us
    ppermute x3, starting transfers between devices, turn(): return lax.ppermute(block, 'seq', route)  12 us
    pallas_call x3, Pallas kernels, attention(): pl.pallas_call(functools.partial(attend, distances, chunk, state is not N...  10.4 us
    ppermute x4, waiting for transfers between devices, shift(): lax.ppermute(block, AXES, [(i, i + distance) for i in range(n - distance)])  7.62 us
    add x1, other arithmetic, over(): lax.pad(first, zero, ((0, n, 0), (0, 0, 0)))  1.07 us
    dynamic_slice x1, local copies, waits for them, and re-layouts, pair(): lax.dynamic_slice_in_dim(held, jnp.where(wraps, 2 * tok, 0), 4 * tok, 0)  1.05 us
    unnamed x8, local copies, waits for them, and re-layouts  0.95 us
  transfers between devices with their start and end apart: 7, of which 1 were waited for; matrix products, arithmetic and copies ran while one was open for 2% of the time, Pallas kernels for 16%

commit v1 on v0

--- a/solution.py
+++ b/solution.py
@@ -18,9 +18,10 @@
 MASKED = -1e30
 
 
-def shift(block, distance):
+def shift(block, distance, columns=SIDE):
     n = lax.axis_size(AXES)
-    return lax.ppermute(block, AXES, [(i, i + distance) for i in range(n - distance)])
+    route = [(i, i + distance) for i in range(n - distance) if i % SIDE < columns]
+    return lax.ppermute(block, AXES, route)
 
 
 def attend(distances, chunk, merge, final, *refs):
@@ -181,7 +182,7 @@
     kv8 = shift(kv, 2 * SIDE)
     across = turn(kv, 2)
     across4 = shift(across, SIDE)
-    across8 = shift(across, 2 * SIDE)
+    across8 = shift(across, 2 * SIDE, 2)
     held = jnp.concatenate([kv, kv4, kv8], axis=0)
 
     def pair(columns):

time: 47.2 us -> 47.2 us (level)
  no operation moved by 1% of the time
where the time goes in v1:
time: 47.2 us; the launch traced here: 46.9 us
  starting transfers between devices  25.6 us (54%)
  Pallas kernels  10.4 us (22%)
  waiting for transfers between devices  7.63 us (16%)
  local copies, waits for them, and re-layouts  2 us (4%)
  other arithmetic  1.13 us (2%)
    ppermute x4, starting transfers between devices, shift(): return lax.ppermute(block, AXES, route)  13.6 us
    ppermute x3, starting transfers between devices, turn(): return lax.ppermute(block, 'seq', route)  12 us
    pallas_call x3, Pallas kernels, attention(): pl.pallas_call(functools.partial(attend, distances, chunk, state is not N...  10.4 us
    ppermute x4, waiting for transfers between devices, shift(): return lax.ppermute(block, AXES, route)  7.62 us
    add x1, other arithmetic, over(): lax.pad(first, zero, ((0, n, 0), (0, 0, 0)))  1.07 us
    dynamic_slice x1, local copies, waits for them, and re-layouts, pair(): lax.dynamic_slice_in_dim(held, jnp.where(wraps, 2 * tok, 0), 4 * tok, 0)  1.05 us
    unnamed x8, local copies, waits for them, and re-layouts  0.95 us
  transfers between devices with their start and end apart: 7, of which 1 were waited for; matrix products, arithmetic and copies ran while one was open for 2% of the time, Pallas kernels for 16%

profile of v1, /device:TPU:8, one launch (start us, length us, event | category | flops | bytes accessed | tf_op | source)
XLA Modules:
  0.0 46.9 jit_solution(17140289907837965230)
XLA Ops:
  0.0 0.0 copy-start.3
  0.0 0.0 copy-start
  0.0 1.1 %pad_add_fusion.refs_2_ = bf16[256,512]{1,0:T(8,128)(2,1)S(1)} fusion(bf16[128,512]{1,0:T(8,128)(2,1)} %param.6, bf16[128,512]{1,0:T(8,128)(2,1)} %param.5), kind=kLoop, calls=%fused_computation.1 | loop fusion | flops 524288 | bytes 524288 | tf_op jit(solution)/shard_map/add | solution.py:170
  1.1 3.5 %collective-permute-start.3 = (bf16[256,512]{1,0:T(8,128)(2,1)S(1)}, bf16[256,512]{1,0:T(8,128)(2,1)S(1)}, u32[]{:S(2)}, u32[]{:S(2)}) collective-permute-start(bf16[256,512]{1,0:T(8,128)(2,1)S(1)} %pad_add_fusion.refs_2_), channel_id=1, source_target_pairs={{0,4},{1,5},{2,6},{3,7},{4,8},{5,9},{6,10},{7,11},{8,12},{9,13},{1... | collective-permute-start | bytes 786440 | tf_op jit(solution)/shard_map/ppermute | solution.py:24
  4.6 2.7 %collective-permute-start.4 = (bf16[256,512]{1,0:T(8,128)(2,1)S(1)}, bf16[256,512]{1,0:T(8,128)(2,1)S(1)}, u32[]{:S(2)}, u32[]{:S(2)}) collective-permute-start(bf16[256,512]{1,0:T(8,128)(2,1)S(1)} %pad_add_fusion.refs_2_), channel_id=1, source_target_pairs={{0,8},{1,9},{2,10},{3,11},{4,12},{5,13},{6,14},{7,15},{8,16},{9,17... | collective-permute-start | bytes 786440 | tf_op jit(solution)/shard_map/ppermute | solution.py:24
  7.2 4.9 %collective-permute-start = (bf16[256,512]{1,0:T(8,128)(2,1)S(1)}, bf16[256,512]{1,0:T(8,128)(2,1)S(1)}, u32[]{:S(2)}, u32[]{:S(2)}) collective-permute-start(bf16[256,512]{1,0:T(8,128)(2,1)S(1)} %pad_add_fusion.refs_2_), channel_id=1, source_target_pairs={{0,2},{1,3},{2,0},{3,1},{4,6},{5,7},{6,4},{7,5},{8,10},{9,11},{10,... | collective-permute-start | bytes 786440 | tf_op jit(solution)/shard_map/ppermute | solution.py:165
  12.2 7.6 %collective-permute-done.3.refs_3_ = bf16[256,512]{1,0:T(8,128)(2,1)S(1)} collective-permute-done((bf16[256,512]{1,0:T(8,128)(2,1)S(1)}, bf16[256,512]{1,0:T(8,128)(2,1)S(1)}, u32[]{:S(2)}, u32[]{:S(2)}) %collective-permute-start.3) | collective-permute-done | bytes 262176 | tf_op jit(solution)/shard_map/ppermute | solution.py:24
  19.8 0.0 collective-permute-done.4.refs_4_
  19.8 0.0 copy-start.1
  19.8 0.1 pad_maximum_fusion
  19.9 1.0 %constant_dynamic-slice_fusion = (bf16[512,512]{1,0:T(8,128)(2,1)}, bf16[512,512]{1,0:T(8,128)(2,1)}) fusion(bf16[768,512]{1,0:T(8,128)(2,1)S(1)} %pad_maximum_fusion, s32[]{:T(128)S(6)} %select_n.18, s32[]{:T(128)S(6)} %select_n.17), kind=kLoop, calls=%fused_computation.2 | loop fusion | bytes 2097160 | tf_op jit(solution)/shard_map/dynamic_slice | solution.py:190
  20.9 1.9 %collective-permute-start.5 = (bf16[512,512]{1,0:T(8,128)(2,1)}, bf16[512,512]{1,0:T(8,128)(2,1)S(1)}, u32[]{:S(2)}, u32[]{:S(2)}) collective-permute-start(bf16[512,512]{1,0:T(8,128)(2,1)} %get-tuple-element.18), channel_id=1, source_target_pairs={{0,1},{1,2},{2,3},{3,0},{4,5},{5,6},{6,7},{7,4},{8,9},{9,10},{10,1... | collective-permute-start | bytes 1572872 | tf_op jit(solution)/shard_map/ppermute | solution.py:165
  22.8 5.1 %collective-permute-start.6 = (bf16[512,512]{1,0:T(8,128)(2,1)}, bf16[512,512]{1,0:T(8,128)(2,1)S(1)}, u32[]{:S(2)}, u32[]{:S(2)}) collective-permute-start(bf16[512,512]{1,0:T(8,128)(2,1)} %get-tuple-element.17), channel_id=1, source_target_pairs={{0,3},{1,0},{2,1},{3,2},{4,7},{5,4},{6,5},{7,6},{8,11},{9,8},{10,9... | collective-permute-start | bytes 1572872 | tf_op jit(solution)/shard_map/ppermute | solution.py:165
  28.0 0.0 copy-done.1
  28.0 0.0 collective-permute-done.refs_3_
  28.0 6.2 %collective-permute-start.1 = (bf16[256,512]{1,0:T(8,128)(2,1)S(1)}, bf16[256,512]{1,0:T(8,128)(2,1)S(1)}, u32[]{:S(2)}, u32[]{:S(2)}) collective-permute-start(bf16[256,512]{1,0:T(8,128)(2,1)S(1)} %collective-permute-done.refs_3_), channel_id=1, source_target_pairs={{0,4},{1,5},{2,6},{3,7},{4,8},{5,9},{6,10},{7,11},{8,12},{9,13},{1... | collective-permute-start | bytes 786440 | tf_op jit(solution)/shard_map/ppermute | solution.py:24
  34.2 1.3 %collective-permute-start.2 = (bf16[256,512]{1,0:T(8,128)(2,1)S(1)}, bf16[256,512]{1,0:T(8,128)(2,1)S(1)}, u32[]{:S(2)}, u32[]{:S(2)}) collective-permute-start(bf16[256,512]{1,0:T(8,128)(2,1)S(1)} %collective-permute-done.refs_3_), channel_id=1, source_target_pairs={{0,8},{1,9},{4,12},{5,13},{8,16},{9,17},{12,20},{13,21},{16,24},{1... | collective-permute-start | bytes 786440 | tf_op jit(solution)/shard_map/ppermute | solution.py:24
  35.5 0.0 copy-done.3
  35.5 0.0 copy-done
  35.5 0.0 copy-start.2
  35.5 0.9 %copy-done.2 = bf16[256,512]{1,0:T(8,128)(2,1)S(1)} copy-done((bf16[256,512]{1,0:T(8,128)(2,1)S(1)}, bf16[256,512]{1,0:T(8,128)(2,1)}, u32[]{:S(2)}) %copy-start.2) | copy-done | bytes 262168
  36.5 3.3 %shard_map.46 = (f32[128,4096]{1,0:T(8,128)S(1)}, f32[128,4096]{1,0:T(8,128)S(1)}, f32[128,4096]{1,0:T(8,128)S(1)}) custom-call(s32[1,128]{1,0:T(1,128)S(1)} %subtract_bitcast_fusion.refs_0_, bf16[128,4096]{1,0:T(8,128)(2,1)S(1)} %copy-done, bf16[256,512]{1,0:T(8,128)(2,1)S(1)} %pad_add_fusion.refs_2_, bf16[256,512]{1,0:T(8,128)(2,1)S(1)} %collective-permute-done.3.refs_3_, ...), custom_call_target="tpu_custom_call" | custom-call | flops 805306368 | bytes 3670016 | tf_op jit(solution)/shard_map/pallas_call | solution.py:146
  39.8 0.0 collective-permute-done.5.refs_2_
  39.9 0.0 collective-permute-done.6.refs_3_
  39.9 4.1 %shard_map.47 = (f32[128,4096]{1,0:T(8,128)S(1)}, f32[128,4096]{1,0:T(8,128)S(1)}, f32[128,4096]{1,0:T(8,128)S(1)}) custom-call(s32[1,128]{1,0:T(1,128)S(1)} %subtract_bitcast_fusion.refs_0_, bf16[128,4096]{1,0:T(8,128)(2,1)S(1)} %copy-done, ...), custom_call_target="tpu_custom_call", output_to_operand_aliasing={{0}: (4, {}), {1}: (5, {}), {2}: (6, {})} | custom-call | flops 1073741824 | bytes 4194304 | tf_op jit(solution)/shard_map/pallas_call | solution.py:146
  44.0 0.0 collective-permute-done.1.refs_4_
  44.0 0.0 collective-permute-done.2.refs_5_
  44.0 2.9 %shard_map.48 = bf16[128,4096]{1,0:T(8,128)(2,1)} custom-call(s32[1,128]{1,0:T(1,128)S(1)} %subtract_bitcast_fusion.refs_0_, bf16[128,4096]{1,0:T(8,128)(2,1)S(1)} %copy-done, s32[1]{0:T(128)} %bitcast.1.refs_2_, bf16[256,512]{1,0:T(8,128)(2,1)S(1)} %collective-permute-done.refs_3_, bf16[256,512]{1,0:T(8,128)(2,1)S(1)} %collective-permute-done.1.refs_4_, ...), custom_call_target="tpu_custom_call" | custom-call | flops 536870912 | bytes 3145728 | tf_op jit(solution)/shard_map/pallas_call | solution.py:146
  (1 shorter events, 0.0 us)
Async XLA Ops:
  0.0 35.5 %copy-start.3 = (s32[128]{0:T(128)S(1)}, s32[128]{0:T(128)}, u32[]{:S(2)}) copy-start(s32[128]{0:T(128)} %param.7) | copy-start | bytes 1540
  0.0 35.5 %copy-start = (bf16[128,4096]{1,0:T(8,128)(2,1)S(1)}, bf16[128,4096]{1,0:T(8,128)(2,1)}, u32[]{:S(2)}) copy-start(bf16[128,4096]{1,0:T(8,128)(2,1)} %refs_1_.5) | copy-start | bytes 3145732
  1.1 18.7 %collective-permute-start.3 = (bf16[256,512]{1,0:T(8,128)(2,1)S(1)}, bf16[256,512]{1,0:T(8,128)(2,1)S(1)}, u32[]{:S(2)}, u32[]{:S(2)}) collective-permute-start(bf16[256,512]{1,0:T(8,128)(2,1)S(1)} %pad_add_fusion.refs_2_), channel_id=1, source_target_pairs={{0,4},{1,5},{2,6},{3,7},{4,8},{5,9},{6,10},{7,11},{8,12},{9,13},{1... | collective-permute-start | bytes 786440 | tf_op jit(solution)/shard_map/ppermute | solution.py:24
  4.6 15.2 %collective-permute-start.4 = (bf16[256,512]{1,0:T(8,128)(2,1)S(1)}, bf16[256,512]{1,0:T(8,128)(2,1)S(1)}, u32[]{:S(2)}, u32[]{:S(2)}) collective-permute-start(bf16[256,512]{1,0:T(8,128)(2,1)S(1)} %pad_add_fusion.refs_2_), channel_id=1, source_target_pairs={{0,8},{1,9},{2,10},{3,11},{4,12},{5,13},{6,14},{7,15},{8,16},{9,17... | collective-permute-start | bytes 786440 | tf_op jit(solution)/shard_map/ppermute | solution.py:24
  7.2 20.8 %collective-permute-start = (bf16[256,512]{1,0:T(8,128)(2,1)S(1)}, bf16[256,512]{1,0:T(8,128)(2,1)S(1)}, u32[]{:S(2)}, u32[]{:S(2)}) collective-permute-start(bf16[256,512]{1,0:T(8,128)(2,1)S(1)} %pad_add_fusion.refs_2_), channel_id=1, source_target_pairs={{0,2},{1,3},{2,0},{3,1},{4,6},{5,7},{6,4},{7,5},{8,10},{9,11},{10,... | collective-permute-start | bytes 786440 | tf_op jit(solution)/shard_map/ppermute | solution.py:165
  19.8 8.2 %copy-start.1 = (bf16[256,512]{1,0:T(8,128)(2,1)}, bf16[256,512]{1,0:T(8,128)(2,1)S(1)}, u32[]{:S(2)}) copy-start(bf16[256,512]{1,0:T(8,128)(2,1)S(1)} %collective-permute-done.4.refs_4_) | copy-start | bytes 786436
  20.9 18.9 %collective-permute-start.5 = (bf16[512,512]{1,0:T(8,128)(2,1)}, bf16[512,512]{1,0:T(8,128)(2,1)S(1)}, u32[]{:S(2)}, u32[]{:S(2)}) collective-permute-start(bf16[512,512]{1,0:T(8,128)(2,1)} %get-tuple-element.18), channel_id=1, source_target_pairs={{0,1},{1,2},{2,3},{3,0},{4,5},{5,6},{6,7},{7,4},{8,9},{9,10},{10,1... | collective-permute-start | bytes 1572872 | tf_op jit(solution)/shard_map/ppermute | solution.py:165
  22.8 17.0 %collective-permute-start.6 = (bf16[512,512]{1,0:T(8,128)(2,1)}, bf16[512,512]{1,0:T(8,128)(2,1)S(1)}, u32[]{:S(2)}, u32[]{:S(2)}) collective-permute-start(bf16[512,512]{1,0:T(8,128)(2,1)} %get-tuple-element.17), channel_id=1, source_target_pairs={{0,3},{1,0},{2,1},{3,2},{4,7},{5,4},{6,5},{7,6},{8,11},{9,8},{10,9... | collective-permute-start | bytes 1572872 | tf_op jit(solution)/shard_map/ppermute | solution.py:165
  28.0 16.0 %collective-permute-start.1 = (bf16[256,512]{1,0:T(8,128)(2,1)S(1)}, bf16[256,512]{1,0:T(8,128)(2,1)S(1)}, u32[]{:S(2)}, u32[]{:S(2)}) collective-permute-start(bf16[256,512]{1,0:T(8,128)(2,1)S(1)} %collective-permute-done.refs_3_), channel_id=1, source_target_pairs={{0,4},{1,5},{2,6},{3,7},{4,8},{5,9},{6,10},{7,11},{8,12},{9,13},{1... | collective-permute-start | bytes 786440 | tf_op jit(solution)/shard_map/ppermute | solution.py:24
  34.2 9.8 %collective-permute-start.2 = (bf16[256,512]{1,0:T(8,128)(2,1)S(1)}, bf16[256,512]{1,0:T(8,128)(2,1)S(1)}, u32[]{:S(2)}, u32[]{:S(2)}) collective-permute-start(bf16[256,512]{1,0:T(8,128)(2,1)S(1)} %collective-permute-done.refs_3_), channel_id=1, source_target_pairs={{0,8},{1,9},{4,12},{5,13},{8,16},{9,17},{12,20},{13,21},{16,24},{1... | collective-permute-start | bytes 786440 | tf_op jit(solution)/shard_map/ppermute | solution.py:24
  35.5 1.0 %copy-start.2 = (bf16[256,512]{1,0:T(8,128)(2,1)S(1)}, bf16[256,512]{1,0:T(8,128)(2,1)}, u32[]{:S(2)}) copy-start(bf16[256,512]{1,0:T(8,128)(2,1)} %copy-done.1) | copy-start | bytes 786436

commit v2 on v1

--- a/solution.py
+++ b/solution.py
@@ -181,8 +181,8 @@
     kv4 = shift(kv, SIDE)
     kv8 = shift(kv, 2 * SIDE)
     across = turn(kv, 2)
+    across8 = shift(across, 2 * SIDE, 2)
     across4 = shift(across, SIDE)
-    across8 = shift(across, 2 * SIDE, 2)
     held = jnp.concatenate([kv, kv4, kv8], axis=0)
 
     def pair(columns):
@@ -194,9 +194,9 @@
     starts = starts - me * tok
     state = attention(starts, queries, [kv, kv4, kv8], [(0,), (4,), (8,)])
     state = attention(starts, queries, [kv15, kv37], [(1, 5), (3, 7)], state=state, chunk=2)
-    early = (column < 2).astype(jnp.int32).reshape(1)
+    late = (column >= 2).astype(jnp.int32).reshape(1)
     return attention(
-        starts, queries, [across, across4, across8], [(2,), (6,)], state=state, flag=early
+        starts, queries, [across8, across4, across], [(6,), (2,)], state=state, flag=late
     )
 
 

time: 47.2 us -> 47.9 us (1.015)
  starting transfers between devices: 25.6 us -> 26.2 us
    ppermute x4, starting transfers between devices: 13.6 us -> 14.2 us  [shift(): return lax.ppermute(block, AXES, route)]
where the time goes in v2:
time: 47.9 us; the launch traced here: 47.6 us
  starting transfers between devices  26.2 us (55%)
  Pallas kernels  10.4 us (22%)
  waiting for transfers between devices  7.63 us (16%)
  local copies, waits for them, and re-layouts  2 us (4%)
  other arithmetic  1.13 us (2%)
    ppermute x4, starting transfers between devices, shift(): return lax.ppermute(block, AXES, route)  14.2 us
    ppermute x3, starting transfers between devices, turn(): return lax.ppermute(block, 'seq', route)  12 us
    pallas_call x3, Pallas kernels, attention(): pl.pallas_call(functools.partial(attend, distances, chunk, state is not N...  10.4 us
    ppermute x4, waiting for transfers between devices, shift(): return lax.ppermute(block, AXES, route)  7.62 us
    add x1, other arithmetic, over(): lax.pad(first, zero, ((0, n, 0), (0, 0, 0)))  1.07 us
    dynamic_slice x1, local copies, waits for them, and re-layouts, pair(): lax.dynamic_slice_in_dim(held, jnp.where(wraps, 2 * tok, 0), 4 * tok, 0)  1.05 us
  transfers between devices with their start and end apart: 7, of which 1 were waited for; matrix products, arithmetic and copies ran while one was open for 2% of the time, Pallas kernels for 16%

profile of v2, /device:TPU:8, one launch (start us, length us, event | category | flops | bytes accessed | tf_op | source)
XLA Modules:
  0.0 47.6 jit_solution(15739117395001518964)
XLA Ops:
  0.0 0.0 copy-start.3
  0.0 0.0 copy-start
  0.0 1.1 %pad_add_fusion.refs_2_ = bf16[256,512]{1,0:T(8,128)(2,1)S(1)} fusion(bf16[128,512]{1,0:T(8,128)(2,1)} %param.6, bf16[128,512]{1,0:T(8,128)(2,1)} %param.5), kind=kLoop, calls=%fused_computation.1 | loop fusion | flops 524288 | bytes 524288 | tf_op jit(solution)/shard_map/add | solution.py:170
  1.1 3.5 %collective-permute-start.3 = (bf16[256,512]{1,0:T(8,128)(2,1)S(1)}, bf16[256,512]{1,0:T(8,128)(2,1)S(1)}, u32[]{:S(2)}, u32[]{:S(2)}) collective-permute-start(bf16[256,512]{1,0:T(8,128)(2,1)S(1)} %pad_add_fusion.refs_2_), channel_id=1, source_target_pairs={{0,4},{1,5},{2,6},{3,7},{4,8},{5,9},{6,10},{7,11},{8,12},{9,13},{1... | collective-permute-start | bytes 786440 | tf_op jit(solution)/shard_map/ppermute | solution.py:24
  4.6 2.7 %collective-permute-start.4 = (bf16[256,512]{1,0:T(8,128)(2,1)S(1)}, bf16[256,512]{1,0:T(8,128)(2,1)S(1)}, u32[]{:S(2)}, u32[]{:S(2)}) collective-permute-start(bf16[256,512]{1,0:T(8,128)(2,1)S(1)} %pad_add_fusion.refs_2_), channel_id=1, source_target_pairs={{0,8},{1,9},{2,10},{3,11},{4,12},{5,13},{6,14},{7,15},{8,16},{9,17... | collective-permute-start | bytes 786440 | tf_op jit(solution)/shard_map/ppermute | solution.py:24
  7.2 4.9 %collective-permute-start = (bf16[256,512]{1,0:T(8,128)(2,1)S(1)}, bf16[256,512]{1,0:T(8,128)(2,1)S(1)}, u32[]{:S(2)}, u32[]{:S(2)}) collective-permute-start(bf16[256,512]{1,0:T(8,128)(2,1)S(1)} %pad_add_fusion.refs_2_), channel_id=1, source_target_pairs={{0,2},{1,3},{2,0},{3,1},{4,6},{5,7},{6,4},{7,5},{8,10},{9,11},{10,... | collective-permute-start | bytes 786440 | tf_op jit(solution)/shard_map/ppermute | solution.py:165
  12.2 7.6 %collective-permute-done.3.refs_3_ = bf16[256,512]{1,0:T(8,128)(2,1)S(1)} collective-permute-done((bf16[256,512]{1,0:T(8,128)(2,1)S(1)}, bf16[256,512]{1,0:T(8,128)(2,1)S(1)}, u32[]{:S(2)}, u32[]{:S(2)}) %collective-permute-start.3) | collective-permute-done | bytes 262176 | tf_op jit(solution)/shard_map/ppermute | solution.py:24
  19.8 0.0 collective-permute-done.4.refs_4_
  19.8 0.0 copy-start.1
  19.8 0.1 pad_maximum_fusion
  19.9 1.0 %constant_dynamic-slice_fusion = (bf16[512,512]{1,0:T(8,128)(2,1)}, bf16[512,512]{1,0:T(8,128)(2,1)}) fusion(bf16[768,512]{1,0:T(8,128)(2,1)S(1)} %pad_maximum_fusion, s32[]{:T(128)S(6)} %select_n.18, s32[]{:T(128)S(6)} %select_n.17), kind=kLoop, calls=%fused_computation.2 | loop fusion | bytes 2097160 | tf_op jit(solution)/shard_map/dynamic_slice | solution.py:190
  20.9 1.9 %collective-permute-start.5 = (bf16[512,512]{1,0:T(8,128)(2,1)}, bf16[512,512]{1,0:T(8,128)(2,1)S(1)}, u32[]{:S(2)}, u32[]{:S(2)}) collective-permute-start(bf16[512,512]{1,0:T(8,128)(2,1)} %get-tuple-element.18), channel_id=1, source_target_pairs={{0,1},{1,2},{2,3},{3,0},{4,5},{5,6},{6,7},{7,4},{8,9},{9,10},{10,1... | collective-permute-start | bytes 1572872 | tf_op jit(solution)/shard_map/ppermute | solution.py:165
  22.8 5.1 %collective-permute-start.6 = (bf16[512,512]{1,0:T(8,128)(2,1)}, bf16[512,512]{1,0:T(8,128)(2,1)S(1)}, u32[]{:S(2)}, u32[]{:S(2)}) collective-permute-start(bf16[512,512]{1,0:T(8,128)(2,1)} %get-tuple-element.17), channel_id=1, source_target_pairs={{0,3},{1,0},{2,1},{3,2},{4,7},{5,4},{6,5},{7,6},{8,11},{9,8},{10,9... | collective-permute-start | bytes 1572872 | tf_op jit(solution)/shard_map/ppermute | solution.py:165
  28.0 0.0 copy-done.1
  28.0 0.0 collective-permute-done.refs_5_
  28.0 1.3 %collective-permute-start.1 = (bf16[256,512]{1,0:T(8,128)(2,1)S(1)}, bf16[256,512]{1,0:T(8,128)(2,1)S(1)}, u32[]{:S(2)}, u32[]{:S(2)}) collective-permute-start(bf16[256,512]{1,0:T(8,128)(2,1)S(1)} %collective-permute-done.refs_5_), channel_id=1, source_target_pairs={{0,8},{1,9},{4,12},{5,13},{8,16},{9,17},{12,20},{13,21},{16,24},{1... | collective-permute-start | bytes 786440 | tf_op jit(solution)/shard_map/ppermute | solution.py:24
  29.3 6.8 %collective-permute-start.2 = (bf16[256,512]{1,0:T(8,128)(2,1)S(1)}, bf16[256,512]{1,0:T(8,128)(2,1)S(1)}, u32[]{:S(2)}, u32[]{:S(2)}) collective-permute-start(bf16[256,512]{1,0:T(8,128)(2,1)S(1)} %collective-permute-done.refs_5_), channel_id=1, source_target_pairs={{0,4},{1,5},{2,6},{3,7},{4,8},{5,9},{6,10},{7,11},{8,12},{9,13},{1... | collective-permute-start | bytes 786440 | tf_op jit(solution)/shard_map/ppermute | solution.py:24
  36.1 0.0 copy-done.3
  36.1 0.0 copy-done
  36.1 0.0 copy-start.2
  36.2 0.9 %copy-done.2 = bf16[256,512]{1,0:T(8,128)(2,1)S(1)} copy-done((bf16[256,512]{1,0:T(8,128)(2,1)S(1)}, bf16[256,512]{1,0:T(8,128)(2,1)}, u32[]{:S(2)}) %copy-start.2) | copy-done | bytes 262168
  37.1 3.3 %shard_map.46 = (f32[128,4096]{1,0:T(8,128)S(1)}, f32[128,4096]{1,0:T(8,128)S(1)}, f32[128,4096]{1,0:T(8,128)S(1)}) custom-call(s32[1,128]{1,0:T(1,128)S(1)} %subtract_bitcast_fusion.refs_0_, bf16[128,4096]{1,0:T(8,128)(2,1)S(1)} %copy-done, bf16[256,512]{1,0:T(8,128)(2,1)S(1)} %pad_add_fusion.refs_2_, bf16[256,512]{1,0:T(8,128)(2,1)S(1)} %collective-permute-done.3.refs_3_, ...), custom_call_target="tpu_custom_call" | custom-call | flops 805306368 | bytes 3670016 | tf_op jit(solution)/shard_map/pallas_call | solution.py:146
  40.5 0.0 collective-permute-done.5.refs_2_
  40.5 0.0 collective-permute-done.6.refs_3_
  40.5 4.1 %shard_map.47 = (f32[128,4096]{1,0:T(8,128)S(1)}, f32[128,4096]{1,0:T(8,128)S(1)}, f32[128,4096]{1,0:T(8,128)S(1)}) custom-call(s32[1,128]{1,0:T(1,128)S(1)} %subtract_bitcast_fusion.refs_0_, bf16[128,4096]{1,0:T(8,128)(2,1)S(1)} %copy-done, ...), custom_call_target="tpu_custom_call", output_to_operand_aliasing={{0}: (4, {}), {1}: (5, {}), {2}: (6, {})} | custom-call | flops 1073741824 | bytes 4194304 | tf_op jit(solution)/shard_map/pallas_call | solution.py:146
  44.6 0.0 collective-permute-done.1.refs_3_
  44.6 0.0 collective-permute-done.2.refs_4_
  44.6 2.9 %shard_map.48 = bf16[128,4096]{1,0:T(8,128)(2,1)} custom-call(s32[1,128]{1,0:T(1,128)S(1)} %subtract_bitcast_fusion.refs_0_, bf16[128,4096]{1,0:T(8,128)(2,1)S(1)} %copy-done, s32[1]{0:T(128)} %bitcast.1.refs_2_, bf16[256,512]{1,0:T(8,128)(2,1)S(1)} %collective-permute-done.1.refs_3_, bf16[256,512]{1,0:T(8,128)(2,1)S(1)} %collective-permute-done.2.refs_4_, ...), custom_call_target="tpu_custom_call" | custom-call | flops 536870912 | bytes 3145728 | tf_op jit(solution)/shard_map/pallas_call | solution.py:146
  (1 shorter events, 0.0 us)
Async XLA Ops:
  0.0 36.1 %copy-start.3 = (s32[128]{0:T(128)S(1)}, s32[128]{0:T(128)}, u32[]{:S(2)}) copy-start(s32[128]{0:T(128)} %param.7) | copy-start | bytes 1540
  0.0 36.1 %copy-start = (bf16[128,4096]{1,0:T(8,128)(2,1)S(1)}, bf16[128,4096]{1,0:T(8,128)(2,1)}, u32[]{:S(2)}) copy-start(bf16[128,4096]{1,0:T(8,128)(2,1)} %refs_1_.5) | copy-start | bytes 3145732
  1.1 18.7 %collective-permute-start.3 = (bf16[256,512]{1,0:T(8,128)(2,1)S(1)}, bf16[256,512]{1,0:T(8,128)(2,1)S(1)}, u32[]{:S(2)}, u32[]{:S(2)}) collective-permute-start(bf16[256,512]{1,0:T(8,128)(2,1)S(1)} %pad_add_fusion.refs_2_), channel_id=1, source_target_pairs={{0,4},{1,5},{2,6},{3,7},{4,8},{5,9},{6,10},{7,11},{8,12},{9,13},{1... | collective-permute-start | bytes 786440 | tf_op jit(solution)/shard_map/ppermute | solution.py:24
  4.6 15.2 %collective-permute-start.4 = (bf16[256,512]{1,0:T(8,128)(2,1)S(1)}, bf16[256,512]{1,0:T(8,128)(2,1)S(1)}, u32[]{:S(2)}, u32[]{:S(2)}) collective-permute-start(bf16[256,512]{1,0:T(8,128)(2,1)S(1)} %pad_add_fusion.refs_2_), channel_id=1, source_target_pairs={{0,8},{1,9},{2,10},{3,11},{4,12},{5,13},{6,14},{7,15},{8,16},{9,17... | collective-permute-start | bytes 786440 | tf_op jit(solution)/shard_map/ppermute | solution.py:24
  7.2 20.8 %collective-permute-start = (bf16[256,512]{1,0:T(8,128)(2,1)S(1)}, bf16[256,512]{1,0:T(8,128)(2,1)S(1)}, u32[]{:S(2)}, u32[]{:S(2)}) collective-permute-start(bf16[256,512]{1,0:T(8,128)(2,1)S(1)} %pad_add_fusion.refs_2_), channel_id=1, source_target_pairs={{0,2},{1,3},{2,0},{3,1},{4,6},{5,7},{6,4},{7,5},{8,10},{9,11},{10,... | collective-permute-start | bytes 786440 | tf_op jit(solution)/shard_map/ppermute | solution.py:165
  19.8 8.2 %copy-start.1 = (bf16[256,512]{1,0:T(8,128)(2,1)}, bf16[256,512]{1,0:T(8,128)(2,1)S(1)}, u32[]{:S(2)}) copy-start(bf16[256,512]{1,0:T(8,128)(2,1)S(1)} %collective-permute-done.4.refs_4_) | copy-start | bytes 786436
  20.9 19.5 %collective-permute-start.5 = (bf16[512,512]{1,0:T(8,128)(2,1)}, bf16[512,512]{1,0:T(8,128)(2,1)S(1)}, u32[]{:S(2)}, u32[]{:S(2)}) collective-permute-start(bf16[512,512]{1,0:T(8,128)(2,1)} %get-tuple-element.18), channel_id=1, source_target_pairs={{0,1},{1,2},{2,3},{3,0},{4,5},{5,6},{6,7},{7,4},{8,9},{9,10},{10,1... | collective-permute-start | bytes 1572872 | tf_op jit(solution)/shard_map/ppermute | solution.py:165
  22.8 17.6 %collective-permute-start.6 = (bf16[512,512]{1,0:T(8,128)(2,1)}, bf16[512,512]{1,0:T(8,128)(2,1)S(1)}, u32[]{:S(2)}, u32[]{:S(2)}) collective-permute-start(bf16[512,512]{1,0:T(8,128)(2,1)} %get-tuple-element.17), channel_id=1, source_target_pairs={{0,3},{1,0},{2,1},{3,2},{4,7},{5,4},{6,5},{7,6},{8,11},{9,8},{10,9... | collective-permute-start | bytes 1572872 | tf_op jit(solution)/shard_map/ppermute | solution.py:165
  28.0 16.6 %collective-permute-start.1 = (bf16[256,512]{1,0:T(8,128)(2,1)S(1)}, bf16[256,512]{1,0:T(8,128)(2,1)S(1)}, u32[]{:S(2)}, u32[]{:S(2)}) collective-permute-start(bf16[256,512]{1,0:T(8,128)(2,1)S(1)} %collective-permute-done.refs_5_), channel_id=1, source_target_pairs={{0,8},{1,9},{4,12},{5,13},{8,16},{9,17},{12,20},{13,21},{16,24},{1... | collective-permute-start | bytes 786440 | tf_op jit(solution)/shard_map/ppermute | solution.py:24
  29.3 15.3 %collective-permute-start.2 = (bf16[256,512]{1,0:T(8,128)(2,1)S(1)}, bf16[256,512]{1,0:T(8,128)(2,1)S(1)}, u32[]{:S(2)}, u32[]{:S(2)}) collective-permute-start(bf16[256,512]{1,0:T(8,128)(2,1)S(1)} %collective-permute-done.refs_5_), channel_id=1, source_target_pairs={{0,4},{1,5},{2,6},{3,7},{4,8},{5,9},{6,10},{7,11},{8,12},{9,13},{1... | collective-permute-start | bytes 786440 | tf_op jit(solution)/shard_map/ppermute | solution.py:24
  36.1 1.0 %copy-start.2 = (bf16[256,512]{1,0:T(8,128)(2,1)S(1)}, bf16[256,512]{1,0:T(8,128)(2,1)}, u32[]{:S(2)}) copy-start(bf16[256,512]{1,0:T(8,128)(2,1)} %copy-done.1) | copy-start | bytes 786436

commit v3 on v1

--- a/solution.py
+++ b/solution.py
@@ -193,7 +193,7 @@
     kv37 = turn(pair(3), 3)
     starts = starts - me * tok
     state = attention(starts, queries, [kv, kv4, kv8], [(0,), (4,), (8,)])
-    state = attention(starts, queries, [kv15, kv37], [(1, 5), (3, 7)], state=state, chunk=2)
+    state = attention(starts, queries, [kv15, kv37], [(1, 5), (3, 7)], state=state, chunk=1)
     early = (column < 2).astype(jnp.int32).reshape(1)
     return attention(
         starts, queries, [across, across4, across8], [(2,), (6,)], state=state, flag=early

time: 47.2 us -> 47.4 us (level)
  no operation moved by 1% of the time
where the time goes in v3:
time: 47.4 us; the launch traced here: 47.1 us
  starting transfers between devices  25.6 us (54%)
  Pallas kernels  10.6 us (22%)
  waiting for transfers between devices  7.63 us (16%)
  local copies, waits for them, and re-layouts  2 us (4%)
  other arithmetic  1.13 us (2%)
    ppermute x4, starting transfers between devices, shift(): return lax.ppermute(block, AXES, route)  13.6 us
    ppermute x3, starting transfers between devices, turn(): return lax.ppermute(block, 'seq', route)  12 us
    pallas_call x3, Pallas kernels, attention(): pl.pallas_call(functools.partial(attend, distances, chunk, state is not N...  10.6 us
    ppermute x4, waiting for transfers between devices, shift(): return lax.ppermute(block, AXES, route)  7.62 us
    add x1, other arithmetic, over(): lax.pad(first, zero, ((0, n, 0), (0, 0, 0)))  1.07 us
    dynamic_slice x1, local copies, waits for them, and re-layouts, pair(): lax.dynamic_slice_in_dim(held, jnp.where(wraps, 2 * tok, 0), 4 * tok, 0)  1.05 us
    unnamed x8, local copies, waits for them, and re-layouts  0.95 us
  transfers between devices with their start and end apart: 7, of which 1 were waited for; matrix products, arithmetic and copies ran while one was open for 2% of the time, Pallas kernels for 16%

profile of v3, /device:TPU:8, one launch (start us, length us, event | category | flops | bytes accessed | tf_op | source)
XLA Modules:
  0.0 47.1 jit_solution(18099766579259211526)
XLA Ops:
  0.0 0.0 copy-start.3
  0.0 0.0 copy-start
  0.0 1.1 %pad_add_fusion.refs_2_ = bf16[256,512]{1,0:T(8,128)(2,1)S(1)} fusion(bf16[128,512]{1,0:T(8,128)(2,1)} %param.6, bf16[128,512]{1,0:T(8,128)(2,1)} %param.5), kind=kLoop, calls=%fused_computation.1 | loop fusion | flops 524288 | bytes 524288 | tf_op jit(solution)/shard_map/add | solution.py:170
  1.1 3.5 %collective-permute-start.3 = (bf16[256,512]{1,0:T(8,128)(2,1)S(1)}, bf16[256,512]{1,0:T(8,128)(2,1)S(1)}, u32[]{:S(2)}, u32[]{:S(2)}) collective-permute-start(bf16[256,512]{1,0:T(8,128)(2,1)S(1)} %pad_add_fusion.refs_2_), channel_id=1, source_target_pairs={{0,4},{1,5},{2,6},{3,7},{4,8},{5,9},{6,10},{7,11},{8,12},{9,13},{1... | collective-permute-start | bytes 786440 | tf_op jit(solution)/shard_map/ppermute | solution.py:24
  4.6 2.7 %collective-permute-start.4 = (bf16[256,512]{1,0:T(8,128)(2,1)S(1)}, bf16[256,512]{1,0:T(8,128)(2,1)S(1)}, u32[]{:S(2)}, u32[]{:S(2)}) collective-permute-start(bf16[256,512]{1,0:T(8,128)(2,1)S(1)} %pad_add_fusion.refs_2_), channel_id=1, source_target_pairs={{0,8},{1,9},{2,10},{3,11},{4,12},{5,13},{6,14},{7,15},{8,16},{9,17... | collective-permute-start | bytes 786440 | tf_op jit(solution)/shard_map/ppermute | solution.py:24
  7.2 4.9 %collective-permute-start = (bf16[256,512]{1,0:T(8,128)(2,1)S(1)}, bf16[256,512]{1,0:T(8,128)(2,1)S(1)}, u32[]{:S(2)}, u32[]{:S(2)}) collective-permute-start(bf16[256,512]{1,0:T(8,128)(2,1)S(1)} %pad_add_fusion.refs_2_), channel_id=1, source_target_pairs={{0,2},{1,3},{2,0},{3,1},{4,6},{5,7},{6,4},{7,5},{8,10},{9,11},{10,... | collective-permute-start | bytes 786440 | tf_op jit(solution)/shard_map/ppermute | solution.py:165
  12.2 7.6 %collective-permute-done.3.refs_3_ = bf16[256,512]{1,0:T(8,128)(2,1)S(1)} collective-permute-done((bf16[256,512]{1,0:T(8,128)(2,1)S(1)}, bf16[256,512]{1,0:T(8,128)(2,1)S(1)}, u32[]{:S(2)}, u32[]{:S(2)}) %collective-permute-start.3) | collective-permute-done | bytes 262176 | tf_op jit(solution)/shard_map/ppermute | solution.py:24
  19.8 0.0 collective-permute-done.4.refs_4_
  19.8 0.0 copy-start.1
  19.8 0.1 pad_maximum_fusion
  19.9 1.0 %constant_dynamic-slice_fusion = (bf16[512,512]{1,0:T(8,128)(2,1)}, bf16[512,512]{1,0:T(8,128)(2,1)}) fusion(bf16[768,512]{1,0:T(8,128)(2,1)S(1)} %pad_maximum_fusion, s32[]{:T(128)S(6)} %select_n.18, s32[]{:T(128)S(6)} %select_n.17), kind=kLoop, calls=%fused_computation.2 | loop fusion | bytes 2097160 | tf_op jit(solution)/shard_map/dynamic_slice | solution.py:190
  20.9 1.9 %collective-permute-start.5 = (bf16[512,512]{1,0:T(8,128)(2,1)}, bf16[512,512]{1,0:T(8,128)(2,1)S(1)}, u32[]{:S(2)}, u32[]{:S(2)}) collective-permute-start(bf16[512,512]{1,0:T(8,128)(2,1)} %get-tuple-element.18), channel_id=1, source_target_pairs={{0,1},{1,2},{2,3},{3,0},{4,5},{5,6},{6,7},{7,4},{8,9},{9,10},{10,1... | collective-permute-start | bytes 1572872 | tf_op jit(solution)/shard_map/ppermute | solution.py:165
  22.8 5.1 %collective-permute-start.6 = (bf16[512,512]{1,0:T(8,128)(2,1)}, bf16[512,512]{1,0:T(8,128)(2,1)S(1)}, u32[]{:S(2)}, u32[]{:S(2)}) collective-permute-start(bf16[512,512]{1,0:T(8,128)(2,1)} %get-tuple-element.17), channel_id=1, source_target_pairs={{0,3},{1,0},{2,1},{3,2},{4,7},{5,4},{6,5},{7,6},{8,11},{9,8},{10,9... | collective-permute-start | bytes 1572872 | tf_op jit(solution)/shard_map/ppermute | solution.py:165
  28.0 0.0 copy-done.1
  28.0 0.0 collective-permute-done.refs_3_
  28.0 6.2 %collective-permute-start.1 = (bf16[256,512]{1,0:T(8,128)(2,1)S(1)}, bf16[256,512]{1,0:T(8,128)(2,1)S(1)}, u32[]{:S(2)}, u32[]{:S(2)}) collective-permute-start(bf16[256,512]{1,0:T(8,128)(2,1)S(1)} %collective-permute-done.refs_3_), channel_id=1, source_target_pairs={{0,4},{1,5},{2,6},{3,7},{4,8},{5,9},{6,10},{7,11},{8,12},{9,13},{1... | collective-permute-start | bytes 786440 | tf_op jit(solution)/shard_map/ppermute | solution.py:24
  34.2 1.3 %collective-permute-start.2 = (bf16[256,512]{1,0:T(8,128)(2,1)S(1)}, bf16[256,512]{1,0:T(8,128)(2,1)S(1)}, u32[]{:S(2)}, u32[]{:S(2)}) collective-permute-start(bf16[256,512]{1,0:T(8,128)(2,1)S(1)} %collective-permute-done.refs_3_), channel_id=1, source_target_pairs={{0,8},{1,9},{4,12},{5,13},{8,16},{9,17},{12,20},{13,21},{16,24},{1... | collective-permute-start | bytes 786440 | tf_op jit(solution)/shard_map/ppermute | solution.py:24
  35.5 0.0 copy-done.3
  35.5 0.0 copy-done
  35.5 0.0 copy-start.2
  35.5 0.9 %copy-done.2 = bf16[256,512]{1,0:T(8,128)(2,1)S(1)} copy-done((bf16[256,512]{1,0:T(8,128)(2,1)S(1)}, bf16[256,512]{1,0:T(8,128)(2,1)}, u32[]{:S(2)}) %copy-start.2) | copy-done | bytes 262168
  36.5 3.3 %shard_map.46 = (f32[128,4096]{1,0:T(8,128)S(1)}, f32[128,4096]{1,0:T(8,128)S(1)}, f32[128,4096]{1,0:T(8,128)S(1)}) custom-call(s32[1,128]{1,0:T(1,128)S(1)} %subtract_bitcast_fusion.refs_0_, bf16[128,4096]{1,0:T(8,128)(2,1)S(1)} %copy-done, bf16[256,512]{1,0:T(8,128)(2,1)S(1)} %pad_add_fusion.refs_2_, bf16[256,512]{1,0:T(8,128)(2,1)S(1)} %collective-permute-done.3.refs_3_, ...), custom_call_target="tpu_custom_call" | custom-call | flops 805306368 | bytes 3670016 | tf_op jit(solution)/shard_map/pallas_call | solution.py:146
  39.8 0.0 collective-permute-done.5.refs_2_
  39.9 0.0 collective-permute-done.6.refs_3_
  39.9 4.3 %shard_map.47 = (f32[128,4096]{1,0:T(8,128)S(1)}, f32[128,4096]{1,0:T(8,128)S(1)}, f32[128,4096]{1,0:T(8,128)S(1)}) custom-call(s32[1,128]{1,0:T(1,128)S(1)} %subtract_bitcast_fusion.refs_0_, bf16[128,4096]{1,0:T(8,128)(2,1)S(1)} %copy-done, ...), custom_call_target="tpu_custom_call", output_to_operand_aliasing={{0}: (4, {}), {1}: (5, {}), {2}: (6, {})} | custom-call | flops 1073741824 | bytes 4194304 | tf_op jit(solution)/shard_map/pallas_call | solution.py:146
  44.2 0.0 collective-permute-done.1.refs_4_
  44.2 0.0 collective-permute-done.2.refs_5_
  44.2 2.9 %shard_map.48 = bf16[128,4096]{1,0:T(8,128)(2,1)} custom-call(s32[1,128]{1,0:T(1,128)S(1)} %subtract_bitcast_fusion.refs_0_, bf16[128,4096]{1,0:T(8,128)(2,1)S(1)} %copy-done, s32[1]{0:T(128)} %bitcast.1.refs_2_, bf16[256,512]{1,0:T(8,128)(2,1)S(1)} %collective-permute-done.refs_3_, bf16[256,512]{1,0:T(8,128)(2,1)S(1)} %collective-permute-done.1.refs_4_, ...), custom_call_target="tpu_custom_call" | custom-call | flops 536870912 | bytes 3145728 | tf_op jit(solution)/shard_map/pallas_call | solution.py:146
  (1 shorter events, 0.0 us)
Async XLA Ops:
  0.0 35.5 %copy-start.3 = (s32[128]{0:T(128)S(1)}, s32[128]{0:T(128)}, u32[]{:S(2)}) copy-start(s32[128]{0:T(128)} %param.7) | copy-start | bytes 1540
  0.0 35.5 %copy-start = (bf16[128,4096]{1,0:T(8,128)(2,1)S(1)}, bf16[128,4096]{1,0:T(8,128)(2,1)}, u32[]{:S(2)}) copy-start(bf16[128,4096]{1,0:T(8,128)(2,1)} %refs_1_.5) | copy-start | bytes 3145732
  1.1 18.7 %collective-permute-start.3 = (bf16[256,512]{1,0:T(8,128)(2,1)S(1)}, bf16[256,512]{1,0:T(8,128)(2,1)S(1)}, u32[]{:S(2)}, u32[]{:S(2)}) collective-permute-start(bf16[256,512]{1,0:T(8,128)(2,1)S(1)} %pad_add_fusion.refs_2_), channel_id=1, source_target_pairs={{0,4},{1,5},{2,6},{3,7},{4,8},{5,9},{6,10},{7,11},{8,12},{9,13},{1... | collective-permute-start | bytes 786440 | tf_op jit(solution)/shard_map/ppermute | solution.py:24
  4.6 15.2 %collective-permute-start.4 = (bf16[256,512]{1,0:T(8,128)(2,1)S(1)}, bf16[256,512]{1,0:T(8,128)(2,1)S(1)}, u32[]{:S(2)}, u32[]{:S(2)}) collective-permute-start(bf16[256,512]{1,0:T(8,128)(2,1)S(1)} %pad_add_fusion.refs_2_), channel_id=1, source_target_pairs={{0,8},{1,9},{2,10},{3,11},{4,12},{5,13},{6,14},{7,15},{8,16},{9,17... | collective-permute-start | bytes 786440 | tf_op jit(solution)/shard_map/ppermute | solution.py:24
  7.2 20.8 %collective-permute-start = (bf16[256,512]{1,0:T(8,128)(2,1)S(1)}, bf16[256,512]{1,0:T(8,128)(2,1)S(1)}, u32[]{:S(2)}, u32[]{:S(2)}) collective-permute-start(bf16[256,512]{1,0:T(8,128)(2,1)S(1)} %pad_add_fusion.refs_2_), channel_id=1, source_target_pairs={{0,2},{1,3},{2,0},{3,1},{4,6},{5,7},{6,4},{7,5},{8,10},{9,11},{10,... | collective-permute-start | bytes 786440 | tf_op jit(solution)/shard_map/ppermute | solution.py:165
  19.8 8.2 %copy-start.1 = (bf16[256,512]{1,0:T(8,128)(2,1)}, bf16[256,512]{1,0:T(8,128)(2,1)S(1)}, u32[]{:S(2)}) copy-start(bf16[256,512]{1,0:T(8,128)(2,1)S(1)} %collective-permute-done.4.refs_4_) | copy-start | bytes 786436
  20.9 18.9 %collective-permute-start.5 = (bf16[512,512]{1,0:T(8,128)(2,1)}, bf16[512,512]{1,0:T(8,128)(2,1)S(1)}, u32[]{:S(2)}, u32[]{:S(2)}) collective-permute-start(bf16[512,512]{1,0:T(8,128)(2,1)} %get-tuple-element.18), channel_id=1, source_target_pairs={{0,1},{1,2},{2,3},{3,0},{4,5},{5,6},{6,7},{7,4},{8,9},{9,10},{10,1... | collective-permute-start | bytes 1572872 | tf_op jit(solution)/shard_map/ppermute | solution.py:165
  22.8 17.0 %collective-permute-start.6 = (bf16[512,512]{1,0:T(8,128)(2,1)}, bf16[512,512]{1,0:T(8,128)(2,1)S(1)}, u32[]{:S(2)}, u32[]{:S(2)}) collective-permute-start(bf16[512,512]{1,0:T(8,128)(2,1)} %get-tuple-element.17), channel_id=1, source_target_pairs={{0,3},{1,0},{2,1},{3,2},{4,7},{5,4},{6,5},{7,6},{8,11},{9,8},{10,9... | collective-permute-start | bytes 1572872 | tf_op jit(solution)/shard_map/ppermute | solution.py:165
  28.0 16.2 %collective-permute-start.1 = (bf16[256,512]{1,0:T(8,128)(2,1)S(1)}, bf16[256,512]{1,0:T(8,128)(2,1)S(1)}, u32[]{:S(2)}, u32[]{:S(2)}) collective-permute-start(bf16[256,512]{1,0:T(8,128)(2,1)S(1)} %collective-permute-done.refs_3_), channel_id=1, source_target_pairs={{0,4},{1,5},{2,6},{3,7},{4,8},{5,9},{6,10},{7,11},{8,12},{9,13},{1... | collective-permute-start | bytes 786440 | tf_op jit(solution)/shard_map/ppermute | solution.py:24
  34.2 10.0 %collective-permute-start.2 = (bf16[256,512]{1,0:T(8,128)(2,1)S(1)}, bf16[256,512]{1,0:T(8,128)(2,1)S(1)}, u32[]{:S(2)}, u32[]{:S(2)}) collective-permute-start(bf16[256,512]{1,0:T(8,128)(2,1)S(1)} %collective-permute-done.refs_3_), channel_id=1, source_target_pairs={{0,8},{1,9},{4,12},{5,13},{8,16},{9,17},{12,20},{13,21},{16,24},{1... | collective-permute-start | bytes 786440 | tf_op jit(solution)/shard_map/ppermute | solution.py:24
  35.5 1.0 %copy-start.2 = (bf16[256,512]{1,0:T(8,128)(2,1)S(1)}, bf16[256,512]{1,0:T(8,128)(2,1)}, u32[]{:S(2)}) copy-start(bf16[256,512]{1,0:T(8,128)(2,1)} %copy-done.1) | copy-start | bytes 786436
